TPU v7x, 256 devices: a whole 4x4x8 slice. The times are simulated.
256 devices in a mesh: dp: 16 (over z, y_hi), seq: 16 (over y_lo, x, core).
Axes of the slice: x: 4, y: 4 (y_hi: 2, y_lo: 2; y = y_hi * 2 + y_lo), z: 8, core: 2. Of those that a mesh axis runs over, the one named last changes fastest.
Arguments:
- q_proj: bfloat16 [32, 2048, 4096], P('dp', 'seq'), may hold values from -6 to 6
- k_proj: bfloat16 [32, 2048, 1024], P('dp', 'seq'), may hold values from -6 to 6
- v_proj: bfloat16 [32, 2048, 1024], P('dp', 'seq'), may hold values from -6 to 6
- hidden_in: bfloat16 [32, 2048, 4096], P('dp', 'seq'), may hold values from -6 to 6
- out_weight: bfloat16 [4096, 4096], P('seq'), may hold values from -0.09375 to 0.09375
- doc_lengths: int32 [32], P('dp'), may hold values from 512 to 2048, as said below
- positive: int32 [32], replicated, may hold values from 0 to 31, as said below
Outputs:
- passage_contrast_cost: float32 [32], P('dp')
- wo_grad: float32 [4096, 4096], P('seq', 'dp')
Inputs may be any that keep to these rules, and one draw needn't show every extreme that they name: `doc_lengths`: some document has exactly 2048 valid positions. `positive`: never the document itself.
All inputs are finite; a program needn't handle non-finite values.
Results may differ from a plain program's by a relative error of at most 0.00055.
Values may be sent and summed in bfloat16 or wider, within the bound.
A program may use at most 128 MiB of HBM per device.

v0:
```python
import math

import jax
import jax.numpy as jnp
from jax import lax
from jax.sharding import PartitionSpec as P

HEAD_SIZE = 128


logit_divisor = 0.05
norm_eps = 1e-06


def attend_block(rows_of_query, rows_of_key, rows_of_value):
    item_count, sequence_length, query_cols = rows_of_query.shape
    local_kv = rows_of_key.shape[2] // HEAD_SIZE
    local_q = query_cols // HEAD_SIZE
    head_groups = local_q // local_kv
    block_rows = min(512, sequence_length)
    heads_of_query = rows_of_query.reshape(
        item_count, sequence_length, local_kv, head_groups, HEAD_SIZE
    )
    heads_of_key = rows_of_key.reshape(item_count, sequence_length, local_kv, HEAD_SIZE)
    heads_of_value = rows_of_value.reshape(item_count, sequence_length, local_kv, HEAD_SIZE)
    outputs = []
    for block_index in range(sequence_length // block_rows):
        row_start = block_index * block_rows
        row_stop = row_start + block_rows
        scores = jnp.einsum(
            "nqhgd,nkhd->nhgqk",
            heads_of_query[:, row_start:row_stop],
            heads_of_key[:, :row_stop],
            preferred_element_type=jnp.float32,
        ) / math.sqrt(HEAD_SIZE)
        visible = jnp.arange(row_start, row_stop)[:, None] >= jnp.arange(row_stop)[None, :]
        scores = jnp.where(visible, scores, -1e30)
        row_peak = jnp.max(scores, axis=-1, keepdims=True)
        raised_logits = jnp.exp(scores - row_peak)
        cumulative_sums = jnp.sum(raised_logits, axis=-1, keepdims=True)
        rounded = raised_logits.astype(jnp.bfloat16)
        mixed_out = (
            jnp.einsum(
                "nhgqk,nkhd->nhgqd",
                rounded,
                heads_of_value[:, :row_stop],
                preferred_element_type=jnp.float32,
            )
            / cumulative_sums
        )
        mixed_out = jnp.transpose(mixed_out, (0, 3, 1, 2, 4)).reshape(
            item_count, block_rows, query_cols
        )
        outputs.append(mixed_out.astype(jnp.bfloat16))
    return jnp.concatenate(outputs, 1)


def contrast(source_pooled, full_pooled_matrix, targets, row_first):
    passage_similarities = (
        jnp.dot(source_pooled, full_pooled_matrix.T, precision=lax.Precision.HIGHEST)
        / logit_divisor
    )
    target_slot = jnp.arange(full_pooled_matrix.shape[0])[None, :]
    source_slot = row_first + jnp.arange(source_pooled.shape[0])[:, None]
    raised_logits = jnp.exp(passage_similarities - 1.0 / logit_divisor) * (
        target_slot != source_slot
    ).astype(jnp.float32)
    cumulative_sums = jnp.sum(raised_logits, axis=1, keepdims=True)
    chosen_entries = (target_slot == targets[:, None]).astype(jnp.float32)
    passage_contrast_cost = (
        jnp.log(cumulative_sums[:, 0])
        + 1.0 / logit_divisor
        - jnp.sum(passage_similarities * chosen_entries, axis=1)
    )
    return (passage_contrast_cost, raised_logits / cumulative_sums - chosen_entries)


def shards(q_proj, k_proj, v_proj, hidden_in, out_weight, doc_lengths, positive):
    seq_count = lax.axis_size("seq")
    seq_rank = lax.axis_index("seq")
    docs_here, tok_here, query_width = q_proj.shape
    kv_heads = k_proj.shape[2] // HEAD_SIZE
    repeats = max(1, seq_count // kv_heads)

    def widen_heads(source):
        shaped = source.reshape(docs_here, tok_here, kv_heads, 1, HEAD_SIZE)
        spread = jnp.broadcast_to(shaped, (docs_here, tok_here, kv_heads, repeats, HEAD_SIZE))
        return spread.reshape(docs_here, tok_here, kv_heads * repeats * HEAD_SIZE)

    key_send = widen_heads(k_proj)
    value_send = widen_heads(v_proj)
    rows_of_query = lax.all_to_all(q_proj, "seq", split_axis=2, concat_axis=1, tiled=True)
    rows_of_key = lax.all_to_all(key_send, "seq", split_axis=2, concat_axis=1, tiled=True)
    rows_of_value = lax.all_to_all(value_send, "seq", split_axis=2, concat_axis=1, tiled=True)
    attended = attend_block(rows_of_query, rows_of_key, rows_of_value)
    sequence_length = attended.shape[1]
    counts = doc_lengths.astype(jnp.float32)[:, None]
    valid_full = (jnp.arange(sequence_length)[None, :] < doc_lengths[:, None]).astype(jnp.bfloat16)
    pooled = (
        jnp.einsum("dt,dtc->dc", valid_full, attended, preferred_element_type=jnp.float32) / counts
    )
    local_places = seq_rank * tok_here + jnp.arange(tok_here)
    valid_here = (local_places[None, :] < doc_lengths[:, None]).astype(jnp.bfloat16)
    residual = (
        jnp.einsum("dt,dtc->dc", valid_here, hidden_in, preferred_element_type=jnp.float32) / counts
    )
    partial_embed = residual + jnp.dot(
        pooled, out_weight.astype(jnp.float32), precision=lax.Precision.HIGHEST
    )
    raw_embed = lax.psum(partial_embed, "seq")
    gathered = lax.all_gather(raw_embed, "dp", axis=0, tiled=True)
    whole_unit = gathered * lax.rsqrt(
        jnp.sum(gathered * gathered, axis=1, keepdims=True) + norm_eps
    )
    squares = jnp.sum(raw_embed * raw_embed, axis=1, keepdims=True) + norm_eps
    inv_norm = lax.rsqrt(squares)
    unit_embed = raw_embed * inv_norm
    row_first = lax.axis_index("dp") * docs_here
    own_targets = lax.dynamic_slice_in_dim(positive, row_first, docs_here, 0)
    passage_contrast_cost, grad_rows = contrast(unit_embed, whole_unit, own_targets, row_first)
    source_slice = jnp.dot(grad_rows, whole_unit, precision=lax.Precision.HIGHEST)
    col_terms = jnp.dot(grad_rows.T, unit_embed, precision=lax.Precision.HIGHEST)
    col_summed = lax.psum(col_terms, "dp")
    target_holder = lax.dynamic_slice_in_dim(col_summed, row_first, docs_here, 0)
    pooled_derivative = (source_slice + target_holder) / logit_divisor
    along_grad = jnp.sum(raw_embed * pooled_derivative, axis=1, keepdims=True)
    grad_raw = (pooled_derivative - raw_embed * along_grad / squares) * inv_norm
    grad_terms = jnp.dot(pooled.T, grad_raw, precision=lax.Precision.HIGHEST)
    wo_grad = lax.psum_scatter(grad_terms, "dp", scatter_dimension=1, tiled=True)
    return (passage_contrast_cost, wo_grad)


def solution(mesh):
    return jax.shard_map(
        shards,
        mesh=mesh,
        in_specs=(
            P("dp", "seq", None),
            P("dp", "seq", None),
            P("dp", "seq", None),
            P("dp", "seq", None),
            P("seq", None),
            P("dp"),
            P(),
        ),
        out_specs=(P("dp"), P("seq", "dp")),
        check_vma=False,
    )
```

profile of v0, /device:TPU:1, one launch (start us, length us, event | category | flops | bytes accessed | tf_op | source)
XLA Modules:
  0.0 606.5 jit_solution(10093666250323003257)
XLA Ops:
  7.2 0.0 copy-start
  7.2 1.5 copy.62
  8.6 1.8 broadcast_in_dim.42
  10.4 6.8 %all-to-all-start = ((bf16[2,128,2048]{1,0,2:T(2,128)(2,1)}), bf16[2,128,2048]{1,0,2:T(2,128)(2,1)S(1)}, u32[]{:S(2)}, u32[]{:S(2)}) async-start(bf16[2,128,2048]{1,0,2:T(2,128)(2,1)} %bitcast.221), calls=%async_computation | async-start | bytes 2097152 | tf_op jit(solution)/shard_map/all_to_all | solution.py:93
  17.3 2.0 copy.63
  19.3 13.8 %all-to-all-done = bf16[2,128,2048]{1,0,2:T(2,128)(2,1)S(1)} async-done(((bf16[2,128,2048]{1,0,2:T(2,128)(2,1)}), bf16[2,128,2048]{1,0,2:T(2,128)(2,1)S(1)}, u32[]{:S(2)}, u32[]{:S(2)}) %all-to-all-start) | async-done | bytes 1048608 | tf_op jit(solution)/shard_map/all_to_all | solution.py:93
  33.1 3.2 broadcast_in_dim.45
  36.3 4.8 all-to-all-start.2
  41.1 6.2 %copy.31 = bf16[2,128,4096]{1,0,2:T(2,128)(2,1)} copy(bf16[2,128,4096]{2,1,0:T(8,128)(2,1)} %param.7) | data formatting | bytes 4194304 | tf_op args[0]
  47.3 0.1 iota_compare_fusion.3
  47.4 0.0 copy-done.12
  47.4 0.1 compare_bitcast_fusion.1
  47.5 9.7 %all-to-all-done.2 = bf16[2,128,2048]{1,0,2:T(2,128)(2,1)} async-done(((bf16[2,128,2048]{1,0,2:T(2,128)(2,1)}), bf16[2,128,2048]{1,0,2:T(2,128)(2,1)}, u32[]{:S(2)}, u32[]{:S(2)}) %all-to-all-start.2) | async-done | bytes 1048608 | tf_op jit(solution)/shard_map/all_to_all | solution.py:94
  57.2 0.0 copy-done.2
  57.2 4.9 all-to-all-start.1
  62.1 0.2 all-reduce.2.cloned.1.call-start
  62.3 0.1 dynamic_slice.6
  62.4 1.2 iota_compare_fusion.2
  63.6 0.4 fusion.72
  64.0 0.1 compare_bitcast_fusion
  64.1 1.5 iota_compare_fusion.1
  65.6 0.8 iota_compare_fusion
  66.4 1.4 copy.35
  67.9 0.7 copy.36
  68.6 1.3 reshape.195
  69.9 1.3 reshape.220
  71.1 0.1 copy.29
  71.3 1.3 copy.30
  72.6 17.0 %all-to-all-done.1 = bf16[2,128,4096]{1,0,2:T(2,128)(2,1)} async-done(((bf16[2,128,4096]{1,0,2:T(2,128)(2,1)}), bf16[2,128,4096]{1,0,2:T(2,128)(2,1)}, u32[]{:S(2)}, u32[]{:S(2)}) %all-to-all-start.1) | async-done | bytes 2097184 | tf_op jit(solution)/shard_map/all_to_all | solution.py:92
  89.6 2.9 copy.77
  92.6 2.3 reshape.191
  94.9 2.1 fusion.24
  97.1 0.1 copy-done.9
  97.2 1.6 fusion.12
  98.8 0.9 fusion.22
  99.7 0.3 copy-done.11
  100.0 2.1 divide_convert_fusion.2
  102.2 2.0 fusion.10
  104.2 3.2 divide_convert_fusion.1
  107.5 2.4 fusion.5
  109.9 2.8 fusion.3
  112.7 4.3 divide_convert_fusion
  117.0 3.8 fusion.2
  120.8 3.7 fusion
  124.6 5.0 fusion.43
  129.6 0.0 copy-start.6
  129.6 0.6 fusion.28
  130.2 0.9 copy-done.6
  131.1 1.0 convolution_add_fusion.1
  132.1 49.8 %psum.14 = f32[2,4096]{1,0:T(2,128)S(1)} all-reduce(f32[2,4096]{1,0:T(2,128)S(1)} %convolution_add_fusion.1), channel_id=1, replica_groups=mesh['dp'=16,'seq'=16] {'seq'}, use_global_device_ids=true, to_apply=%region_8.9 | all-reduce | flops 8192 | bytes 65536 | tf_op jit(solution)/shard_map/psum | solution.py:110
  181.9 0.1 multiply_reduce_fusion.2
  182.0 39.7 %all-gather = f32[16,2,4096]{2,1,0:T(2,128)S(1)} all-gather(f32[1,2,4096]{2,1,0:T(2,128)S(1)} %bitcast.226), channel_id=1, replica_groups=mesh['dp'=16,'seq'=16] {'dp'}, dimensions={0}, use_global_device_ids=true | all-gather | bytes 557056 | tf_op jit(solution)/shard_map/all_gather | solution.py:111
  221.7 0.4 reshape.210
  222.1 0.2 multiply_reduce_fusion
  222.3 0.7 fusion.84
  223.0 1.6 fusion.64
  224.6 0.0 all-reduce.2.cloned.1.call-update
  224.6 0.0 reduce-scatter.2.cloned.1.call-start
  224.6 151.7 %all-reduce.2.cloned.1.call-done = f32[32,4096]{1,0:T(8,128)} async-done(((f32[32,4096]{1,0:T(8,128)}), f32[32,4096]{1,0:T(8,128)}) %all-reduce.2.cloned.1.call-update) | async-done | bytes 524304 | tf_op jit(solution)/shard_map/psum | solution.py:123
  376.3 1.5 multiply_reduce_fusion.1
  377.8 5.3 fusion.62
  383.2 0.0 reduce-scatter.2.cloned.1.call-update
  383.2 0.5 add_subtract_fusion
  383.7 215.9 %reduce-scatter.2.cloned.1.call-done = f32[256,256]{1,0:T(8,128)} async-done(((f32[256,4096]{1,0:T(8,128)}), f32[256,256]{1,0:T(8,128)}) %reduce-scatter.2.cloned.1.call-update) | async-done | bytes 262160 | tf_op jit(solution)/shard_map/reduce_scatter | solution.py:129
  (35 shorter events, 0.1 us)
Async XLA Ops:
  7.2 56.5 %copy-start = (bf16[2,128,4096]{2,1,0:T(8,128)(2,1)S(1)}, bf16[2,128,4096]{2,1,0:T(8,128)(2,1)}, u32[]{:S(2)}) copy-start(bf16[2,128,4096]{2,1,0:T(8,128)(2,1)} %param.10) | copy-start | bytes 6291460
  10.4 22.7 %all-to-all-start = ((bf16[2,128,2048]{1,0,2:T(2,128)(2,1)}), bf16[2,128,2048]{1,0,2:T(2,128)(2,1)S(1)}, u32[]{:S(2)}, u32[]{:S(2)}) async-start(bf16[2,128,2048]{1,0,2:T(2,128)(2,1)} %bitcast.221), calls=%async_computation | async-start | bytes 2097152 | tf_op jit(solution)/shard_map/all_to_all | solution.py:93
  19.3 28.1 %copy-start.12 = (s32[2]{0:T(128)S(1)}, s32[2]{0:T(128)}, u32[]{:S(2)}) copy-start(s32[2]{0:T(128)} %param.12) | copy-start | bytes 28
  33.1 24.1 %copy-start.2 = (bf16[2,128,2048]{1,0,2:T(2,128)(2,1)}, bf16[2,128,2048]{1,0,2:T(2,128)(2,1)S(1)}, u32[]{:S(2)}) copy-start(bf16[2,128,2048]{1,0,2:T(2,128)(2,1)S(1)} %all-to-all-done) | copy-start | bytes 3145732
  36.3 20.9 %all-to-all-start.2 = ((bf16[2,128,2048]{1,0,2:T(2,128)(2,1)}), bf16[2,128,2048]{1,0,2:T(2,128)(2,1)}, u32[]{:S(2)}, u32[]{:S(2)}) async-start(bf16[2,128,2048]{1,0,2:T(2,128)(2,1)} %bitcast.220), calls=%async_computation.2 | async-start | bytes 2097152 | tf_op jit(solution)/shard_map/all_to_all | solution.py:94
  41.1 21.2 %copy-start.13 = (s32[32]{0:T(128)S(1)}, s32[32]{0:T(128)}, u32[]{:S(2)}) copy-start(s32[32]{0:T(128)} %param.13) | copy-start | bytes 388
  57.2 32.4 %all-to-all-start.1 = ((bf16[2,128,4096]{1,0,2:T(2,128)(2,1)}), bf16[2,128,4096]{1,0,2:T(2,128)(2,1)}, u32[]{:S(2)}, u32[]{:S(2)}) async-start(bf16[2,128,4096]{1,0,2:T(2,128)(2,1)} %copy.31), calls=%async_computation.1 | async-start | bytes 4194304 | tf_op jit(solution)/shard_map/all_to_all | solution.py:92
  62.1 314.3 %all-reduce.2.cloned.1.call-start = ((), (), s32[]{:S(2)}) async-start(), calls=%async_computation.4 | async-start | bytes 1048576 | tf_op jit(solution)/shard_map/psum | solution.py:123
  66.4 4.7 copy-start.3
  94.9 2.1 copy-start.5
  94.9 2.1 copy-start.7
  94.9 2.3 copy-start.9
  98.8 1.2 copy-start.11
  104.2 3.3 copy-start.4
  112.7 4.4 copy-start.10
  120.8 3.7 copy-start.8
  124.5 5.0 copy-start.14
  124.5 5.0 copy-start.15
  124.5 5.0 copy-start.16
  129.6 1.6 copy-start.6
  224.6 375.1 %reduce-scatter.2.cloned.1.call-start = ((), (), s32[]{:S(2)}) async-start(), calls=%async_computation.5 | async-start | bytes 4456448 | tf_op jit(solution)/shard_map/reduce_scatter | solution.py:129
  377.8 221.8 %copy-start.1 = (bf16[2,128,4096]{2,1,0:T(8,128)(2,1)S(1)}, bf16[2,128,4096]{2,1,0:T(8,128)(2,1)}, u32[]{:S(2)}) copy-start(bf16[2,128,4096]{2,1,0:T(8,128)(2,1)} %param.10) | copy-start | bytes 6291460
Sparse Core Ops, SparseCore 0:
  224.7 151.5 all-reduce.1
  383.3 216.2 reduce-scatter.1
where the time goes:
time: 611 us; the launch traced here: 606 us
  waiting for transfers between devices  408 us (67%)
  blocking collectives  89.5 us (15%)
  matrix products  35.8 us (6%)
  local copies, waits for them, and re-layouts  27.9 us (5%)
  starting transfers between devices  16.8 us (3%)
  between operations  14.3 us (2%)
  other arithmetic  14 us (2%)
    reduce_scatter x1, waiting for transfers between devices, shards(): lax.psum_scatter(grad_terms, 'dp', scatter_dimension=1, tiled=True)  216 us
    psum x1, waiting for transfers between devices, shards(): col_summed = lax.psum(col_terms, 'dp')  152 us
    psum x1, blocking collectives, shards(): raw_embed = lax.psum(partial_embed, 'seq')  49.8 us
    all_gather x1, blocking collectives, shards(): gathered = lax.all_gather(raw_embed, 'dp', axis=0, tiled=True)  39.7 us
    all_to_all x1, waiting for transfers between devices, shards(): lax.all_to_all(q_proj, 'seq', split_axis=2, concat_axis=1, tiled=True)  17 us
    dot_general x4, matrix products, attend_block(): jnp.einsum('nhgqk,nkhd->nhgqd', rounded, heads_of_value[:, :row_stop], pr...  14.7 us
    all_to_all x1, waiting for transfers between devices, shards(): lax.all_to_all(key_send, 'seq', split_axis=2, concat_axis=1, tiled=True)  13.8 us
  transfers between devices with their start and end apart: 5, of which 5 were waited for; matrix products, arithmetic and copies ran while one was open for 3% of the time, Pallas kernels for 0%

commit v1 on v0

v1 whole, which is shorter than its diff:
```python
import math

import jax
import jax.numpy as jnp
from jax import lax
from jax.experimental import pallas as pl
from jax.experimental.pallas import tpu as pltpu
from jax.sharding import PartitionSpec as P

MESH = pl.DeviceIdType.MESH
F32 = jnp.float32
BF16 = jnp.bfloat16
HIGHEST = lax.Precision.HIGHEST
LANES = 128
TOK = 128
RANKS = 16
HEADS = 4
LEN = 2048
QB = 256
EXP2_SCALE = math.log2(math.e) / math.sqrt(128.0)
INV_TEMP = 20.0
EPS = 1e-06

(K_SEM, Q_SEM, V_SEM, SIB_SEM, RS_SEM, RG_SEM, TG_SEM, PG_SEM, GRAM_SEM, HID_SEM, W_SEM) = (
    0, 1, 5, 6, 7, 8, 9, 10, 11, 12, 13)
N_SEM = 14


def split3(x):
    hi = x.astype(BF16).astype(F32)
    mid = (x - hi).astype(BF16).astype(F32)
    lo = x - hi - mid
    return hi, mid, lo


def kernel(
    q_ref, k_ref, v_ref, hid_ref, wt_ref, len_ref, pos_ref,
    cost_ref, wo_ref,
    qbuf, kbuf, vbuf, hbuf, wbuf, sbuf, wsum, resid,
    sib, rs_out, rs_buf, rtile, rg_buf, tg_buf, ptile, pg_buf, gtile, gram_buf,
    lhs_ref, rt_mat, pa_mat, rg_mat,
    send_sem, recv_sem,
):
    g = lax.axis_index("dp")
    s = lax.axis_index("seq")
    core = s % 2
    col = (s // 2) % 4
    row = s // 8

    def seq_peer(e):
        odd = e % 2
        i = (e // 2) % 4
        dc = 1 - e // 8
        dx = (i + 3 - 2 * odd) % 4
        return ((row + 1 - odd) % 2) * 8 + ((col + dx) % 4) * 2 + (core + dc) % 2

    hid_copy = pltpu.make_async_copy(hid_ref, hbuf, recv_sem.at[HID_SEM])
    hid_copy.start()
    wt_copy = pltpu.make_async_copy(wt_ref, wbuf, recv_sem.at[W_SEM])
    wt_copy.start()

    barrier = pltpu.get_barrier_semaphore()

    def greet(e, c):
        @pl.when(e < RANKS - 1)
        def _():
            pl.semaphore_signal(barrier, inc=1, device_id=(g, seq_peer(e)), device_id_type=MESH)
            pl.semaphore_signal(
                barrier, inc=1, device_id=((g + e + 1) % RANKS, s), device_id_type=MESH)

        @pl.when(jnp.logical_or(s != g, e != g))
        def _():
            pl.semaphore_signal(barrier, inc=1, device_id=(e, g), device_id_type=MESH)

        return c

    lax.fori_loop(0, RANKS, greet, 0)
    pl.semaphore_wait(barrier, 2 * (RANKS - 1) + RANKS - jnp.where(s == g, 1, 0))

    def remote(src, dst, sem, target):
        pltpu.make_async_remote_copy(
            src_ref=src, dst_ref=dst, send_sem=send_sem.at[sem], recv_sem=recv_sem.at[sem],
            device_id=target, device_id_type=MESH,
        ).start()

    def cols(first):
        return pl.ds(pl.multiple_of(first * LANES, LANES), LANES)

    def send_k(e, c):
        t = seq_peer(e)
        remote(k_ref.at[t % 2, :, cols(t // 2)], kbuf.at[s], K_SEM, (g, t))
        return c

    def send_q(h):
        def body(e, c):
            t = seq_peer(e)
            remote(q_ref.at[t % 2, :, cols((t // 2) * HEADS + h)], qbuf.at[h, s], Q_SEM + h, (g, t))
            return c
        return body

    def send_v(e, c):
        t = seq_peer(e)
        remote(v_ref.at[t % 2, :, cols(t // 2)], vbuf.at[s], V_SEM, (g, t))
        return c

    pltpu.make_async_copy(k_ref.at[core, :, cols(s // 2)], kbuf.at[s], recv_sem.at[K_SEM]).start()
    lax.fori_loop(0, RANKS - 1, send_k, 0)

    def send_head(h, c):
        pltpu.make_async_copy(
            q_ref.at[core, :, cols((s // 2) * HEADS + h)], qbuf.at[h, s], recv_sem.at[Q_SEM + h]
        ).start()
        lax.fori_loop(0, RANKS - 1, send_q(h), 0)
        return c

    lax.fori_loop(0, HEADS, send_head, 0)
    pltpu.make_async_copy(v_ref.at[core, :, cols(s // 2)], vbuf.at[s], recv_sem.at[V_SEM]).start()
    lax.fori_loop(0, RANKS - 1, send_v, 0)

    def wait_all(ref, sem):
        pltpu.make_async_copy(ref, ref, sem).wait()

    len0 = len_ref[0]
    len1 = len_ref[1]

    hid_copy.wait()
    place = s * TOK + lax.broadcasted_iota(jnp.int32, (16, TOK), 1)
    ones = jnp.ones((16, TOK), F32)
    zeros = jnp.zeros((16, TOK), F32)
    for doc, length in ((0, len0), (1, len1)):
        mask = jnp.where(place < length, ones, zeros).astype(BF16)
        inv_len = jnp.full((1, 1), 1.0, F32) / jnp.full((1, 1), length, jnp.int32).astype(F32)

        def add_resid(t, c, doc=doc, mask=mask, inv_len=inv_len):
            part = jnp.dot(
                mask, hbuf[doc, :, pl.ds(pl.multiple_of(t * 256, 256), 256)],
                preferred_element_type=F32) * inv_len
            resid[t, doc:doc + 1, :] = part[0:1, 0:LANES]
            resid[t, 2 + doc:3 + doc, :] = part[0:1, LANES:]
            return c

        lax.fori_loop(0, RANKS, add_resid, 0)

    my_len = len_ref[core]

    wait_all(kbuf, recv_sem.at[K_SEM])

    def one_head(h, c):
        wait_all(qbuf.at[h], recv_sem.at[Q_SEM + h])
        for i in range(LEN // QB):
            n = (i + 1) * QB
            nb = n // TOK
            keys = kbuf[0:nb].reshape(n, LANES)
            queries = qbuf[h, 2 * i:2 * i + 2].reshape(QB, LANES)
            sref = sbuf.at[i % 2]
            sref[0:n, :] = lax.dot_general(
                keys, queries, (((1,), (1,)), ((), ())), preferred_element_type=F32)
            diag = sref[n - QB:n, :]
            vis = lax.broadcasted_iota(jnp.int32, (QB, QB), 0) <= lax.broadcasted_iota(
                jnp.int32, (QB, QB), 1)
            sref[n - QB:n, :] = jnp.where(vis, diag, -1e30)
            peak = sref[0:8, :]
            for r in range(8, n, 8):
                peak = jnp.maximum(peak, sref[r:r + 8, :])
            peak = jnp.max(peak, axis=0, keepdims=True)
            total = jnp.zeros((8, QB), F32)
            step = 64
            for r in range(0, n, step):
                e = jnp.exp2((sref[r:r + step, :] - peak) * EXP2_SCALE)
                sref[r:r + step, :] = e
                total = total + jnp.sum(e.reshape(step // 8, 8, QB), axis=0)
            total = jnp.sum(total, axis=0, keepdims=True)
            t_at = i * QB + lax.broadcasted_iota(jnp.int32, (1, QB), 1)
            ratio = jnp.where(t_at < my_len, 1.0 / total, 0.0)
            for r in range(0, n, step):
                e = sref[r:r + step, :] * ratio
                e = e[:, 0:LANES] + e[:, LANES:]
                if r >= n - QB:
                    wsum[r:r + step, :] = e
                else:
                    wsum[r:r + step, :] += e
        lane_ones = jnp.ones((8, LANES), F32)
        w_row = lax.dot_general(
            lane_ones, wsum[...], (((1,), (1,)), ((), ())), precision=HIGHEST,
            preferred_element_type=F32)
        lhs_ref[h] = w_row
        return c

    lax.fori_loop(0, HEADS, one_head, 0)

    wait_all(vbuf, recv_sem.at[V_SEM])
    inv_my_len = jnp.full((1, 1), 1.0, F32) / jnp.full((1, 1), my_len, jnp.int32).astype(F32)
    parts = [split3(lhs_ref[h, 0:1, :]) for h in range(HEADS)]
    lhs = jnp.concatenate(
        [parts[h][p] for p in range(3) for h in range(HEADS)]
        + [jnp.zeros((4, LEN), F32)], axis=0).astype(BF16)
    out = jnp.dot(lhs, vbuf[...].reshape(LEN, LANES), preferred_element_type=F32)
    mine = (out[0:4] + out[4:8] + out[8:12]) * inv_my_len
    mine = jnp.concatenate([mine, jnp.zeros((4, LANES), F32)], axis=0)

    @pl.when(core == 0)
    def _():
        sib[0] = mine
        remote(sib.at[0], sib.at[0], SIB_SEM, (g, s + 1))

    @pl.when(core == 1)
    def _():
        sib[1] = mine
        remote(sib.at[1], sib.at[1], SIB_SEM, (g, s - 1))

    wait_all(sib.at[0], recv_sem.at[SIB_SEM])
    low = core == 0
    doc0 = jnp.where(low, sib[0, 0:2, :], sib[0, 2:4, :])
    doc1 = jnp.where(low, sib[1, 0:2, :], sib[1, 2:4, :])
    both = jnp.concatenate(
        [doc0[0:1], doc1[0:1], doc0[1:2], doc1[1:2], jnp.zeros((4, LANES), F32)], axis=0)
    ptile[...] = both
    pg_buf[g] = both

    pooled = jnp.concatenate([both[0:2], both[2:4]], axis=1)
    hi, mid, lo = split3(pooled)
    lhs2 = jnp.concatenate([hi, mid, lo, jnp.zeros((10, 2 * LANES), F32)], axis=0).astype(BF16)

    wt_copy.wait()

    def project(e, c):
        t = seq_peer(e)
        part = jnp.dot(
            lhs2, wbuf[:, pl.ds(pl.multiple_of(t * 256, 256), 256)], preferred_element_type=F32)
        part = part[0:2] + part[2:4] + part[4:6]
        tile = resid[t]
        tile = jnp.concatenate(
            [tile[0:2] + part[:, 0:LANES], tile[2:4] + part[:, LANES:],
             jnp.zeros((4, LANES), F32)], axis=0)

        @pl.when(e < RANKS - 1)
        def _():
            rs_out[e] = tile
            remote(rs_out.at[e], rs_buf.at[s], RS_SEM, (g, t))

        @pl.when(e == RANKS - 1)
        def _():
            rs_buf[s] = tile

        return c

    lax.fori_loop(0, RANKS, project, 0)

    def send_pooled(e, c):
        remote(ptile, pg_buf.at[g], PG_SEM, ((g + e + 1) % RANKS, s))
        return c

    lax.fori_loop(0, RANKS - 1, send_pooled, 0)

    wait_all(rs_buf.at[pl.ds(0, RANKS - 1)], recv_sem.at[RS_SEM])
    raw = jnp.sum(rs_buf[...], axis=0)
    rtile[...] = raw
    rg_buf[g] = raw

    def send_raw(e, c):
        remote(rtile, rg_buf.at[g], RG_SEM, ((g + e + 1) % RANKS, s))
        return c

    lax.fori_loop(0, RANKS - 1, send_raw, 0)

    @pl.when(s == g)
    def _():
        tg_buf[g] = raw

    def send_cols(e, c):
        @pl.when(jnp.logical_or(s != g, e != s))
        def _():
            remote(rtile, tg_buf.at[g], TG_SEM, (s, e))
        return c

    lax.fori_loop(0, RANKS, send_cols, 0)

    wait_all(rg_buf.at[pl.ds(0, RANKS - 1)], recv_sem.at[RG_SEM])
    for d in range(RANKS):
        for half in range(2):
            piece = rg_buf[d, 2 * half:2 * half + 2, :]
            for rep in range(4):
                rg_mat[32 * rep + 2 * d:32 * rep + 2 * d + 2, half * LANES:(half + 1) * LANES] = piece
    wide = lax.dot_general(
        rg_mat[0:32, :], rg_mat[...], (((1,), (1,)), ((), ())), precision=HIGHEST,
        preferred_element_type=F32)
    lane_group = lax.broadcasted_iota(jnp.int32, (8, LANES), 1) // 32
    packed = jnp.zeros((8, LANES), F32)
    for p in range(4):
        packed = packed + jnp.where(lane_group == p, wide[8 * p:8 * p + 8], 0.0)
    gtile[...] = packed
    gram_buf[s] = packed

    def send_gram(e, c):
        remote(gtile, gram_buf.at[s], GRAM_SEM, (g, seq_peer(e)))
        return c

    lax.fori_loop(0, RANKS - 1, send_gram, 0)

    wait_all(pg_buf.at[pl.ds(0, RANKS - 1)], recv_sem.at[PG_SEM])
    for d in range(RANKS):
        for half in range(2):
            pa_mat[2 * d:2 * d + 2, half * LANES:(half + 1) * LANES] = pg_buf[
                d, 2 * half:2 * half + 2, :]

    @pl.when(s == g)
    def _():
        wait_all(tg_buf.at[pl.ds(0, RANKS - 1)], recv_sem.at[TG_SEM])

    @pl.when(s != g)
    def _():
        wait_all(tg_buf, recv_sem.at[TG_SEM])

    for d in range(RANKS):
        for half in range(2):
            rt_mat[2 * d:2 * d + 2, half * LANES:(half + 1) * LANES] = tg_buf[
                d, 2 * half:2 * half + 2, :]

    wait_all(gram_buf.at[pl.ds(0, RANKS - 1)], recv_sem.at[GRAM_SEM])
    gp = jnp.sum(gram_buf[...], axis=0)
    gram = jnp.concatenate(
        [gp if p == 0 else pltpu.roll(gp, LANES - 32 * p, 1) for p in range(4)], axis=0)
    ri = lax.broadcasted_iota(jnp.int32, (32, LANES), 0)
    ci = lax.broadcasted_iota(jnp.int32, (32, LANES), 1)
    inside = ci < 32
    eye = ri == ci
    gram = jnp.where(inside, gram, 0.0)
    on_diag = jnp.where(eye, gram, 0.0)
    sq_i = jnp.sum(on_diag, axis=1, keepdims=True) + EPS
    sq_j = jnp.sum(on_diag, axis=0, keepdims=True) + EPS
    inv_i = lax.rsqrt(sq_i)
    inv_j = lax.rsqrt(sq_j)
    sims = gram * inv_i * inv_j * INV_TEMP
    raised = jnp.where(jnp.logical_and(inside, jnp.logical_not(eye)), jnp.exp(sims - INV_TEMP), 0.0)
    tot_i = jnp.sum(raised, axis=1, keepdims=True)
    tot_j = jnp.sum(raised, axis=0, keepdims=True)
    tot_j = jnp.where(ci[0:1] < 32, tot_j, 1.0)
    hot_t = jnp.where(jnp.logical_and(ri == pos_ref[...], inside), 1.0, 0.0)
    eye_f = jnp.where(eye, 1.0, 0.0)
    hot = lax.dot_general(
        jnp.where(lax.broadcasted_iota(jnp.int32, (32, LANES), 0)
                  == lax.broadcasted_iota(jnp.int32, (32, LANES), 1), 1.0, 0.0),
        jnp.concatenate([hot_t, jnp.zeros((96, LANES), F32)], axis=0),
        (((1,), (1,)), ((), ())), precision=HIGHEST, preferred_element_type=F32)
    cost = jnp.log(tot_i) + INV_TEMP - jnp.sum(sims * hot, axis=1, keepdims=True)
    both_grad = raised / tot_i + raised / tot_j - hot - hot_t
    weighted = both_grad * inv_j * INV_TEMP
    along = jnp.sum(weighted * gram, axis=1, keepdims=True)
    coef = inv_i * weighted - eye_f * (inv_i * along / sq_i)
    grad_raw = jnp.dot(coef[:, 0:32], rt_mat[...], precision=HIGHEST, preferred_element_type=F32)
    wo_ref[...] = lax.dot_general(
        pa_mat[...], grad_raw, (((0,), (0,)), ((), ())), precision=HIGHEST,
        preferred_element_type=F32)
    doc_at = lax.broadcasted_iota(jnp.int32, (32, 1), 0)
    cost_ref[0] = jnp.sum(jnp.where(doc_at == 2 * g, cost, 0.0))
    cost_ref[1] = jnp.sum(jnp.where(doc_at == 2 * g + 1, cost, 0.0))

    some = RANKS - 1
    wait_all(kbuf.at[pl.ds(0, some)], send_sem.at[K_SEM])
    for h in range(HEADS):
        wait_all(qbuf.at[h, pl.ds(0, some)], send_sem.at[Q_SEM + h])
    wait_all(vbuf.at[pl.ds(0, some)], send_sem.at[V_SEM])
    wait_all(sib.at[0], send_sem.at[SIB_SEM])
    wait_all(rs_buf.at[pl.ds(0, some)], send_sem.at[RS_SEM])
    wait_all(rg_buf.at[pl.ds(0, some)], send_sem.at[RG_SEM])

    @pl.when(s == g)
    def _():
        wait_all(tg_buf.at[pl.ds(0, some)], send_sem.at[TG_SEM])

    @pl.when(s != g)
    def _():
        wait_all(tg_buf, send_sem.at[TG_SEM])

    wait_all(pg_buf.at[pl.ds(0, some)], send_sem.at[PG_SEM])
    wait_all(gram_buf.at[pl.ds(0, some)], send_sem.at[GRAM_SEM])


def shards(q_proj, k_proj, v_proj, hidden_in, out_weight, doc_lengths, positive):
    any_spec = pl.BlockSpec(memory_space=pl.ANY)
    smem = pl.BlockSpec(memory_space=pltpu.SMEM)
    vmem = pl.BlockSpec(memory_space=pltpu.VMEM)
    wide_pos = jnp.pad(positive.reshape(1, 32), ((0, 0), (0, LANES - 32)))
    tile = (RANKS, 8, LANES)
    return pl.pallas_call(
        kernel,
        out_shape=(
            jax.ShapeDtypeStruct((2,), F32),
            jax.ShapeDtypeStruct((256, 256), F32),
        ),
        in_specs=[any_spec] * 5 + [smem, vmem],
        out_specs=(smem, vmem),
        scratch_shapes=[
            pltpu.VMEM((HEADS, RANKS, TOK, LANES), BF16),
            pltpu.VMEM((RANKS, TOK, LANES), BF16),
            pltpu.VMEM((RANKS, TOK, LANES), BF16),
            pltpu.VMEM((2, TOK, 4096), BF16),
            pltpu.VMEM((256, 4096), BF16),
            pltpu.VMEM((2, LEN, QB), F32),
            pltpu.VMEM((LEN, LANES), F32),
            pltpu.VMEM(tile, F32),
            pltpu.VMEM((2, 8, LANES), F32),
            pltpu.VMEM(tile, F32),
            pltpu.VMEM(tile, F32),
            pltpu.VMEM((8, LANES), F32),
            pltpu.VMEM(tile, F32),
            pltpu.VMEM(tile, F32),
            pltpu.VMEM((8, LANES), F32),
            pltpu.VMEM(tile, F32),
            pltpu.VMEM((8, LANES), F32),
            pltpu.VMEM(tile, F32),
            pltpu.VMEM((HEADS, 8, LEN), F32),
            pltpu.VMEM((32, 256), F32),
            pltpu.VMEM((32, 256), F32),
            pltpu.VMEM((128, 256), F32),
            pltpu.SemaphoreType.DMA((N_SEM,)),
            pltpu.SemaphoreType.DMA((N_SEM,)),
        ],
        compiler_params=pltpu.CompilerParams(
            collective_id=0, has_side_effects=True, vmem_limit_bytes=48 * 2**20),
    )(q_proj, k_proj, v_proj, hidden_in, out_weight, doc_lengths, wide_pos)


def solution(mesh):
    return jax.shard_map(
        shards,
        mesh=mesh,
        in_specs=(
            P("dp", "seq", None),
            P("dp", "seq", None),
            P("dp", "seq", None),
            P("dp", "seq", None),
            P("seq", None),
            P("dp"),
            P(),
        ),
        out_specs=(P("dp"), P("seq", "dp")),
        check_vma=False,
    )
```

time: 611 us -> 77.5 us (0.13)
  waiting for transfers between devices: 408 us -> 0 us
  blocking collectives: 89.5 us -> 0 us
  Pallas kernels: 0 us -> 68.8 us
  matrix products: 35.8 us -> 0 us
  local copies, waits for them, and re-layouts: 27.9 us -> 7.79 us
  starting transfers between devices: 16.8 us -> 0 us
  other arithmetic: 14 us -> 0 us
  between operations: 14.3 us -> 0.64 us
    reduce_scatter x1 -> x0, waiting for transfers between devices: 216 us -> none  [shards(): lax.psum_scatter(grad_terms, 'dp', scatter_dimension=1, tiled=True)]
    psum x1 -> x0, waiting for transfers between devices: 152 us -> none  [shards(): col_summed = lax.psum(col_terms, 'dp')]
    pallas_call x0 -> x1, Pallas kernels: none -> 68.8 us  [shards(): pl.pallas_call(kernel, out_shape=(jax.ShapeDtypeStruct((2,), F32), jax.Sh...]
    psum x1 -> x0, blocking collectives: 49.8 us -> none  [shards(): raw_embed = lax.psum(partial_embed, 'seq')]
    all_to_all x3 -> x0, waiting for transfers between devices: 40.5 us -> none  [the longest x1 17 us: shards(): lax.all_to_all(q_proj, 'seq', split_axis=2, concat_axis=1, tiled=True)]
    all_gather x1 -> x0, blocking collectives: 39.7 us -> none  [shards(): gathered = lax.all_gather(raw_embed, 'dp', axis=0, tiled=True)]
    dot_general x15 -> x0, matrix products: 35.8 us -> none  [the longest x4 14.7 us: attend_block(): jnp.einsum('nhgqk,nkhd->nhgqd', rounded, heads_of_value[:, :row_stop], pr...]
    all_to_all x3 -> x0, starting transfers between devices: 16.5 us -> none  [the longest x1 6.83 us: shards(): lax.all_to_all(key_send, 'seq', split_axis=2, concat_axis=1, tiled=True)]
  transfers between devices with their start and end apart: 5 -> 0, of which waited for: 5 -> 0; matrix products, arithmetic and copies ran while one was open for 3% -> 0% of each run, Pallas kernels for 0% -> 0%
where the time goes in v1:
time: 77.5 us; the launch traced here: 77.2 us
  Pallas kernels  68.8 us (89%)
  local copies, waits for them, and re-layouts  7.79 us (10%)
    pallas_call x1, Pallas kernels, shards(): pl.pallas_call(kernel, out_shape=(jax.ShapeDtypeStruct((2,), F32), jax.Sh...  68.8 us
    unnamed x12, local copies, waits for them, and re-layouts  7.13 us

profile of v1, /device:TPU:1, one launch (start us, length us, event | category | flops | bytes accessed | tf_op | source)
XLA Modules:
  0.0 77.2 jit_solution(5575203789933123483)
XLA Ops:
  0.6 0.7 pad.4.pos_ref
  1.3 0.0 copy-start
  1.3 1.6 %copy-done = bf16[2,128,4096]{2,1,0:T(8,128)(2,1)S(1)} copy-done((bf16[2,128,4096]{2,1,0:T(8,128)(2,1)S(1)}, bf16[2,128,4096]{2,1,0:T(8,128)(2,1)}, u32[]{:S(2)}) %copy-start) | copy-done | bytes 2097176
  2.9 0.0 copy-start.1
  2.9 1.6 %copy-done.1 = bf16[2,128,4096]{2,1,0:T(8,128)(2,1)S(1)} copy-done((bf16[2,128,4096]{2,1,0:T(8,128)(2,1)S(1)}, bf16[2,128,4096]{2,1,0:T(8,128)(2,1)}, u32[]{:S(2)}) %copy-start.1) | copy-done | bytes 2097176
  4.5 0.0 copy-start.2
  4.5 1.0 %copy-done.2 = bf16[2,128,1024]{2,1,0:T(8,128)(2,1)S(1)} copy-done((bf16[2,128,1024]{2,1,0:T(8,128)(2,1)S(1)}, bf16[2,128,1024]{2,1,0:T(8,128)(2,1)}, u32[]{:S(2)}) %copy-start.2) | copy-done | bytes 524312
  5.5 0.0 copy-start.3
  5.5 1.0 %copy-done.3 = bf16[2,128,1024]{2,1,0:T(8,128)(2,1)S(1)} copy-done((bf16[2,128,1024]{2,1,0:T(8,128)(2,1)S(1)}, bf16[2,128,1024]{2,1,0:T(8,128)(2,1)}, u32[]{:S(2)}) %copy-start.3) | copy-done | bytes 524312
  6.6 0.0 copy-start.4
  6.6 0.7 copy-done.4
  7.2 68.8 %shard_map.86 = (f32[2]{0:T(128)S(1)}, f32[256,256]{1,0:T(8,128)S(1)}) custom-call(bf16[2,128,4096]{2,1,0:T(8,128)(2,1)S(1)} %copy-done, bf16[2,128,1024]{2,1,0:T(8,128)(2,1)S(1)} %copy-done.2, bf16[2,128,1024]{2,1,0:T(8,128)(2,1)S(1)} %copy-done.3, bf16[2,128,4096]{2,1,0:T(8,128)(2,1)S(1)} %copy-done.1, bf16[256,4096]{1,0:T(8,128)(2,1)} %wt_ref.1, ...), custom_call_target="tpu_custom_call" | custom-call | tf_op jit(solution)/shard_map/pallas_call | solution.py:385
  76.0 0.5 copy.11
  76.5 0.7 copy.12
Async XLA Ops:
  1.3 1.6 %copy-start = (bf16[2,128,4096]{2,1,0:T(8,128)(2,1)S(1)}, bf16[2,128,4096]{2,1,0:T(8,128)(2,1)}, u32[]{:S(2)}) copy-start(bf16[2,128,4096]{2,1,0:T(8,128)(2,1)} %q_ref.1) | copy-start | bytes 6291460
  2.9 1.6 %copy-start.1 = (bf16[2,128,4096]{2,1,0:T(8,128)(2,1)S(1)}, bf16[2,128,4096]{2,1,0:T(8,128)(2,1)}, u32[]{:S(2)}) copy-start(bf16[2,128,4096]{2,1,0:T(8,128)(2,1)} %hid_ref.1) | copy-start | bytes 6291460
  4.5 1.0 %copy-start.2 = (bf16[2,128,1024]{2,1,0:T(8,128)(2,1)S(1)}, bf16[2,128,1024]{2,1,0:T(8,128)(2,1)}, u32[]{:S(2)}) copy-start(bf16[2,128,1024]{2,1,0:T(8,128)(2,1)} %k_ref.1) | copy-start | bytes 1572868
  5.5 1.0 %copy-start.3 = (bf16[2,128,1024]{2,1,0:T(8,128)(2,1)S(1)}, bf16[2,128,1024]{2,1,0:T(8,128)(2,1)}, u32[]{:S(2)}) copy-start(bf16[2,128,1024]{2,1,0:T(8,128)(2,1)} %v_ref.1) | copy-start | bytes 1572868
  6.6 0.7 copy-start.4

commit v2 on v1

v2 whole, which is shorter than its diff:
```python
import math

import jax
import jax.numpy as jnp
from jax import lax
from jax.experimental import pallas as pl
from jax.experimental.pallas import tpu as pltpu
from jax.sharding import PartitionSpec as P

MESH = pl.DeviceIdType.MESH
F32 = jnp.float32
BF16 = jnp.bfloat16
HIGHEST = lax.Precision.HIGHEST
LANES = 128
TOK = 128
RANKS = 16
HEADS = 4
LEN = 2048
QB = 256
EXP2_SCALE = math.log2(math.e) / math.sqrt(128.0)
INV_TEMP = 20.0
EPS = 1e-06

(K_SEM, Q_SEM, V_SEM, SIB_SEM, RS_SEM, RG_SEM, TG_SEM, PG_SEM, GRAM_SEM, HID_SEM, W_SEM,
 K_IN_SEM, Q_IN_SEM, V_IN_SEM, W_IN_SEM) = (0, 1, 5, 6, 7, 8, 9, 10, 11, 12, 13, 14, 15, 16, 17)
N_SEM = 18


def split3(x):
    hi = x.astype(BF16).astype(F32)
    mid = (x - hi).astype(BF16).astype(F32)
    lo = x - hi - mid
    return hi, mid, lo


def kernel(
    q_hbm, k_hbm, v_hbm, hid_ref, wt_ref, len_ref,
    end_ref,
    q_ref, k_ref, v_ref, qbuf, kbuf, vbuf, hbuf, wbuf, sbuf, wsum, resid,
    sib, rs_out, rs_buf, rtile, rg_buf, tg_buf, ptile, pg_buf, gtile, gram_buf,
    lhs_ref, rg_mat,
    send_sem, recv_sem, sync,
):
    g = lax.axis_index("dp")
    s = lax.axis_index("seq")
    core = s % 2
    col = (s // 2) % 4
    row = s // 8

    def seq_peer(e):
        odd = e % 2
        i = (e // 2) % 4
        dc = 1 - e // 8
        dx = (i + 3 - 2 * odd) % 4
        return ((row + 1 - odd) % 2) * 8 + ((col + dx) % 4) * 2 + (core + dc) % 2

    k_copy = pltpu.make_async_copy(k_hbm, k_ref, recv_sem.at[K_IN_SEM])
    k_copy.start()
    q_copy = pltpu.make_async_copy(q_hbm, q_ref, recv_sem.at[Q_IN_SEM])
    q_copy.start()
    v_copy = pltpu.make_async_copy(v_hbm, v_ref, recv_sem.at[V_IN_SEM])
    v_copy.start()
    hid_copy = pltpu.make_async_copy(hid_ref, hbuf, recv_sem.at[HID_SEM])
    hid_copy.start()
    wt_copy = pltpu.make_async_copy(wt_ref, wbuf.at[core], recv_sem.at[W_IN_SEM])
    wt_copy.start()

    z = g // 2
    y_hi = g % 2
    sibling = (g, s + 1 - 2 * core)
    z_next = (((z + 1) % 8) * 2 + y_hi, s)
    z_prev = (((z + 7) % 8) * 2 + y_hi, s)
    far_half = (z * 2 + 1 - y_hi, s)

    def signal(sem, *targets):
        for target in targets:
            pl.semaphore_signal(sem, inc=1, device_id=target, device_id_type=MESH)

    barrier = pltpu.get_barrier_semaphore()
    signal(barrier, far_half, z_next, z_prev)

    def greet(e, c):
        signal(barrier, (g, seq_peer(e)))
        return c

    lax.fori_loop(0, RANKS - 1, greet, 0)
    pl.semaphore_wait(barrier, RANKS + 2)

    def remote(src, dst, sem, target):
        pltpu.make_async_remote_copy(
            src_ref=src, dst_ref=dst, send_sem=send_sem.at[sem], recv_sem=recv_sem.at[sem],
            device_id=target, device_id_type=MESH,
        ).start()

    def cols(first):
        return pl.ds(pl.multiple_of(first * LANES, LANES), LANES)

    def send_k(e, c):
        t = seq_peer(e)
        remote(k_ref.at[t % 2, :, cols(t // 2)], kbuf.at[s], K_SEM, (g, t))
        return c

    def send_q(h):
        def body(e, c):
            t = seq_peer(e)
            remote(q_ref.at[t % 2, :, cols((t // 2) * HEADS + h)], qbuf.at[h, s], Q_SEM + h, (g, t))
            return c
        return body

    def send_v(e, c):
        t = seq_peer(e)
        remote(v_ref.at[t % 2, :, cols(t // 2)], vbuf.at[s], V_SEM, (g, t))
        return c

    k_copy.wait()
    pltpu.make_async_copy(k_ref.at[core, :, cols(s // 2)], kbuf.at[s], recv_sem.at[K_SEM]).start()
    lax.fori_loop(0, RANKS - 1, send_k, 0)

    q_copy.wait()
    v_copy.wait()

    def send_head(h, c):
        pltpu.make_async_copy(
            q_ref.at[core, :, cols((s // 2) * HEADS + h)], qbuf.at[h, s], recv_sem.at[Q_SEM + h]
        ).start()
        lax.fori_loop(0, RANKS - 1, send_q(h), 0)
        return c

    lax.fori_loop(0, HEADS, send_head, 0)
    pltpu.make_async_copy(v_ref.at[core, :, cols(s // 2)], vbuf.at[s], recv_sem.at[V_SEM]).start()
    lax.fori_loop(0, RANKS - 1, send_v, 0)

    wt_copy.wait()
    remote(wbuf.at[core], wbuf.at[core], W_SEM, sibling)

    for r in range(4):
        signal(sync.at[r], z_next, z_prev)
        pl.semaphore_wait(sync.at[r], 2)
    signal(sync.at[4], far_half)
    pl.semaphore_wait(sync.at[4], 1)

    def wait_all(ref, sem):
        pltpu.make_async_copy(ref, ref, sem).wait()

    len0 = len_ref[0]
    len1 = len_ref[1]

    hid_copy.wait()
    place = s * TOK + lax.broadcasted_iota(jnp.int32, (16, TOK), 1)
    ones = jnp.ones((16, TOK), F32)
    zeros = jnp.zeros((16, TOK), F32)
    for doc, length in ((0, len0), (1, len1)):
        mask = jnp.where(place < length, ones, zeros).astype(BF16)
        inv_len = jnp.full((1, 1), 1.0, F32) / jnp.full((1, 1), length, jnp.int32).astype(F32)

        def add_resid(t, c, doc=doc, mask=mask, inv_len=inv_len):
            part = jnp.dot(
                mask, hbuf[doc, :, pl.ds(pl.multiple_of(t * 256, 256), 256)],
                preferred_element_type=F32) * inv_len
            resid[t, doc:doc + 1, :] = part[0:1, 0:LANES]
            resid[t, 2 + doc:3 + doc, :] = part[0:1, LANES:]
            return c

        lax.fori_loop(0, RANKS, add_resid, 0)

    my_len = len_ref[core]

    wait_all(kbuf, recv_sem.at[K_SEM])

    def one_head(h, c):
        wait_all(qbuf.at[h], recv_sem.at[Q_SEM + h])
        for i in range(LEN // QB):
            n = (i + 1) * QB
            nb = n // TOK
            keys = kbuf[0:nb].reshape(n, LANES)
            queries = qbuf[h, 2 * i:2 * i + 2].reshape(QB, LANES)
            sref = sbuf.at[i % 2]
            sref[0:n, :] = lax.dot_general(
                keys, queries, (((1,), (1,)), ((), ())), preferred_element_type=F32)
            diag = sref[n - QB:n, :]
            vis = lax.broadcasted_iota(jnp.int32, (QB, QB), 0) <= lax.broadcasted_iota(
                jnp.int32, (QB, QB), 1)
            sref[n - QB:n, :] = jnp.where(vis, diag, -1e30)
            peak = sref[0:8, :]
            for r in range(8, n, 8):
                peak = jnp.maximum(peak, sref[r:r + 8, :])
            peak = jnp.max(peak, axis=0, keepdims=True)
            total = jnp.zeros((8, QB), F32)
            step = 64
            for r in range(0, n, step):
                e = jnp.exp2((sref[r:r + step, :] - peak) * EXP2_SCALE)
                sref[r:r + step, :] = e
                total = total + jnp.sum(e.reshape(step // 8, 8, QB), axis=0)
            total = jnp.sum(total, axis=0, keepdims=True)
            t_at = i * QB + lax.broadcasted_iota(jnp.int32, (1, QB), 1)
            ratio = jnp.where(t_at < my_len, 1.0 / total, 0.0)
            for r in range(0, n, step):
                e = sref[r:r + step, :] * ratio
                e = e[:, 0:LANES] + e[:, LANES:]
                if r >= n - QB:
                    wsum[r:r + step, :] = e
                else:
                    wsum[r:r + step, :] += e
        lane_ones = jnp.ones((8, LANES), F32)
        w_row = lax.dot_general(
            lane_ones, wsum[...], (((1,), (1,)), ((), ())), precision=HIGHEST,
            preferred_element_type=F32)
        for p, part in enumerate(split3(w_row[0:1])):
            lhs_ref[pl.ds(p * HEADS + h, 1), :] = part
        return c

    lhs_ref[12:16, :] = jnp.zeros((4, LEN), F32)
    lax.fori_loop(0, HEADS, one_head, 0)
    lhs = lhs_ref[...].astype(BF16)

    wait_all(vbuf, recv_sem.at[V_SEM])
    inv_my_len = jnp.full((1, 1), 1.0, F32) / jnp.full((1, 1), my_len, jnp.int32).astype(F32)
    out = jnp.dot(lhs, vbuf[...].reshape(LEN, LANES), preferred_element_type=F32)
    mine = (out[0:4] + out[4:8] + out[8:12]) * inv_my_len

    wide_mine = jnp.concatenate([mine[h:h + 1] for h in range(HEADS)], axis=1)
    lhs2 = jnp.concatenate(
        list(split3(wide_mine)) + [jnp.zeros((13, HEADS * LANES), F32)], axis=0).astype(BF16)
    wait_all(wbuf.at[0], recv_sem.at[W_SEM])
    part = jnp.dot(
        lhs2, wbuf[...].reshape(HEADS * LANES, 4096), preferred_element_type=F32)
    part = part[0:1] + part[1:2] + part[2:3]
    tile_row = lax.broadcasted_iota(jnp.int32, (4, LANES), 0)
    for t in range(RANKS):
        rs_out[t] = resid[t] + jnp.where(
            tile_row == core, part[:, 256 * t:256 * t + LANES],
            jnp.where(tile_row == 2 + core, part[:, 256 * t + LANES:256 * t + 256], 0.0))

    def send_partial(e, c):
        t = seq_peer(e)
        remote(rs_out.at[t], rs_buf.at[y_hi * RANKS + s], RS_SEM, (g, t))
        remote(rs_out.at[t], rs_buf.at[y_hi * RANKS + s], RS_SEM, (z * 2 + 1 - y_hi, t))
        return c

    lax.fori_loop(0, RANKS - 1, send_partial, 0)
    remote(rs_out.at[s], rs_buf.at[y_hi * RANKS + s], RS_SEM, far_half)
    rs_buf[y_hi * RANKS + s] = rs_out[s]

    sib[core] = mine
    remote(sib.at[core], sib.at[core], SIB_SEM, sibling)
    wait_all(sib.at[0], recv_sem.at[SIB_SEM])
    low = core == 0
    doc0 = jnp.where(low, sib[0, 0:2, :], sib[0, 2:4, :])
    doc1 = jnp.where(low, sib[1, 0:2, :], sib[1, 2:4, :])
    both = jnp.concatenate([doc0[0:1], doc1[0:1], doc0[1:2], doc1[1:2]], axis=0)
    ptile[...] = both
    pg_buf[g] = both

    def send_pooled(e, c):
        remote(ptile, pg_buf.at[g], PG_SEM, ((g + e + 1) % RANKS, s))
        return c

    lax.fori_loop(0, RANKS - 1, send_pooled, 0)

    wait_all(rs_buf.at[pl.ds(0, 2 * RANKS - 1)], recv_sem.at[RS_SEM])
    for half in range(2):
        raw = jnp.sum(rs_buf[half * RANKS:(half + 1) * RANKS], axis=0)
        rtile[half] = raw
        rg_buf[z, half] = raw

    def send_raw(e, c):
        remote(rtile, rg_buf.at[z], RG_SEM, (((z + e + 1) % 8) * 2 + y_hi, s))
        return c

    lax.fori_loop(0, 7, send_raw, 0)

    @pl.when(s == g)
    def _():
        tg_buf[g] = rtile[y_hi]

    def send_cols(e, c):
        @pl.when(jnp.logical_or(s != g, e != s))
        def _():
            remote(rtile.at[y_hi], tg_buf.at[g], TG_SEM, (s, e))
        return c

    lax.fori_loop(0, RANKS, send_cols, 0)

    wait_all(rg_buf.at[pl.ds(0, 7)], recv_sem.at[RG_SEM])
    for d in range(RANKS):
        for half in range(2):
            piece = rg_buf[d // 2, d % 2, 2 * half:2 * half + 2, :]
            for rep in range(4):
                rg_mat[32 * rep + 2 * d:32 * rep + 2 * d + 2, half * LANES:(half + 1) * LANES] = piece
    wide = lax.dot_general(
        rg_mat[0:32, :], rg_mat[...], (((1,), (1,)), ((), ())), precision=HIGHEST,
        preferred_element_type=F32)
    lane_group = lax.broadcasted_iota(jnp.int32, (8, LANES), 1) // 32
    packed = jnp.zeros((8, LANES), F32)
    for p in range(4):
        packed = packed + jnp.where(lane_group == p, wide[8 * p:8 * p + 8], 0.0)
    gtile[...] = packed
    gram_buf[s] = packed

    def send_gram(e, c):
        remote(gtile, gram_buf.at[s], GRAM_SEM, (g, seq_peer(e)))
        return c

    lax.fori_loop(0, RANKS - 1, send_gram, 0)

    wait_all(pg_buf.at[pl.ds(0, RANKS - 1)], recv_sem.at[PG_SEM])
    for d in range(RANKS):
        for half in range(2):
            end_ref[2 * d:2 * d + 2, half * LANES:(half + 1) * LANES] = pg_buf[
                d, 2 * half:2 * half + 2, :]

    @pl.when(s == g)
    def _():
        wait_all(tg_buf.at[pl.ds(0, RANKS - 1)], recv_sem.at[TG_SEM])

    @pl.when(s != g)
    def _():
        wait_all(tg_buf, recv_sem.at[TG_SEM])

    for d in range(RANKS):
        for half in range(2):
            end_ref[32 + 2 * d:34 + 2 * d, half * LANES:(half + 1) * LANES] = tg_buf[
                d, 2 * half:2 * half + 2, :]

    wait_all(gram_buf.at[pl.ds(0, RANKS - 1)], recv_sem.at[GRAM_SEM])
    gp = jnp.sum(gram_buf[...], axis=0)
    end_ref[64:72, 0:LANES] = gp
    end_ref[64:72, LANES:] = gp

    some = RANKS - 1
    wait_all(kbuf.at[pl.ds(0, some)], send_sem.at[K_SEM])
    for h in range(HEADS):
        wait_all(qbuf.at[h, pl.ds(0, some)], send_sem.at[Q_SEM + h])
    wait_all(vbuf.at[pl.ds(0, some)], send_sem.at[V_SEM])
    wait_all(sib.at[0], send_sem.at[SIB_SEM])
    wait_all(wbuf.at[0], send_sem.at[W_SEM])
    wait_all(rs_buf.at[pl.ds(0, 2 * RANKS - 1)], send_sem.at[RS_SEM])
    wait_all(rg_buf.at[pl.ds(0, 7)], send_sem.at[RG_SEM])

    @pl.when(s == g)
    def _():
        wait_all(tg_buf.at[pl.ds(0, some)], send_sem.at[TG_SEM])

    @pl.when(s != g)
    def _():
        wait_all(tg_buf, send_sem.at[TG_SEM])

    wait_all(pg_buf.at[pl.ds(0, some)], send_sem.at[PG_SEM])
    wait_all(gram_buf.at[pl.ds(0, some)], send_sem.at[GRAM_SEM])


def finish(end_ref, pos_ref, cost_ref, wo_ref):
    g = lax.axis_index("dp")
    pooled = end_ref[0:32, :]
    raw = end_ref[32:64, :]
    gp = end_ref[64:72, 0:LANES]
    ri = lax.broadcasted_iota(jnp.int32, (32, 32), 0)
    ci = lax.broadcasted_iota(jnp.int32, (32, 32), 1)
    eye = ri == ci
    eye_f = jnp.where(eye, 1.0, 0.0)
    hot_t = jnp.where(ri == pos_ref[...], 1.0, 0.0)
    hot = lax.dot_general(
        eye_f, hot_t, (((1,), (1,)), ((), ())), precision=HIGHEST, preferred_element_type=F32)
    gram = jnp.concatenate(
        [gp if p == 0 else pltpu.roll(gp, LANES - 32 * p, 1) for p in range(4)], axis=0)[:, 0:32]
    on_diag = jnp.where(eye, gram, 0.0)
    sq_i = jnp.sum(on_diag, axis=1, keepdims=True) + EPS
    sq_j = jnp.sum(on_diag, axis=0, keepdims=True) + EPS
    inv_i = lax.rsqrt(sq_i)
    inv_j = lax.rsqrt(sq_j)
    sims = gram * inv_i * inv_j * INV_TEMP
    raised = jnp.where(eye, 0.0, jnp.exp(sims - INV_TEMP))
    tot_i = jnp.sum(raised, axis=1, keepdims=True)
    tot_j = jnp.sum(raised, axis=0, keepdims=True)
    cost = jnp.log(tot_i) + INV_TEMP - jnp.sum(sims * hot, axis=1, keepdims=True)
    both_grad = raised / tot_i + raised / tot_j - hot - hot_t
    weighted = both_grad * inv_j * INV_TEMP
    along = jnp.sum(weighted * gram, axis=1, keepdims=True)
    coef = inv_i * weighted - eye_f * (inv_i * along / sq_i)
    grad_raw = jnp.dot(coef, raw, precision=HIGHEST, preferred_element_type=F32)
    wo_ref[...] = lax.dot_general(
        pooled, grad_raw, (((0,), (0,)), ((), ())), precision=HIGHEST,
        preferred_element_type=F32)
    doc_at = lax.broadcasted_iota(jnp.int32, (32, 1), 0)
    cost_ref[0] = jnp.sum(jnp.where(doc_at == 2 * g, cost, 0.0))
    cost_ref[1] = jnp.sum(jnp.where(doc_at == 2 * g + 1, cost, 0.0))


def shards(q_proj, k_proj, v_proj, hidden_in, out_weight, doc_lengths, positive):
    any_spec = pl.BlockSpec(memory_space=pltpu.HBM)
    smem = pl.BlockSpec(memory_space=pltpu.SMEM)
    vmem = pl.BlockSpec(memory_space=pltpu.VMEM)
    tile = (RANKS, 4, LANES)
    end = pl.pallas_call(
        kernel,
        out_shape=jax.ShapeDtypeStruct((72, 256), F32),
        in_specs=[any_spec] * 5 + [smem],
        out_specs=vmem,
        scratch_shapes=[
            pltpu.VMEM((2, TOK, 4096), BF16),
            pltpu.VMEM((2, TOK, 1024), BF16),
            pltpu.VMEM((2, TOK, 1024), BF16),
            pltpu.VMEM((HEADS, RANKS, TOK, LANES), BF16),
            pltpu.VMEM((RANKS, TOK, LANES), BF16),
            pltpu.VMEM((RANKS, TOK, LANES), BF16),
            pltpu.VMEM((2, TOK, 4096), BF16),
            pltpu.VMEM((2, 256, 4096), BF16),
            pltpu.VMEM((2, LEN, QB), F32),
            pltpu.VMEM((LEN, LANES), F32),
            pltpu.VMEM(tile, F32),
            pltpu.VMEM((2, 4, LANES), F32),
            pltpu.VMEM(tile, F32),
            pltpu.VMEM((2 * RANKS, 4, LANES), F32),
            pltpu.VMEM((2, 4, LANES), F32),
            pltpu.VMEM((8, 2, 4, LANES), F32),
            pltpu.VMEM(tile, F32),
            pltpu.VMEM((4, LANES), F32),
            pltpu.VMEM(tile, F32),
            pltpu.VMEM((8, LANES), F32),
            pltpu.VMEM((RANKS, 8, LANES), F32),
            pltpu.VMEM((16, LEN), F32),
            pltpu.VMEM((128, 256), F32),
            pltpu.SemaphoreType.DMA((N_SEM,)),
            pltpu.SemaphoreType.DMA((N_SEM,)),
            pltpu.SemaphoreType.REGULAR((5,)),
        ],
        compiler_params=pltpu.CompilerParams(
            collective_id=0, has_side_effects=True, vmem_limit_bytes=60 * 2**20),
    )(q_proj, k_proj, v_proj, hidden_in, out_weight, doc_lengths)
    return pl.pallas_call(
        finish,
        out_shape=(
            jax.ShapeDtypeStruct((2,), F32),
            jax.ShapeDtypeStruct((256, 256), F32),
        ),
        in_specs=[vmem] * 2,
        out_specs=(smem, vmem),
        compiler_params=pltpu.CompilerParams(vmem_limit_bytes=60 * 2**20),
    )(end, positive.reshape(1, 32))


def solution(mesh):
    return jax.shard_map(
        shards,
        mesh=mesh,
        in_specs=(
            P("dp", "seq", None),
            P("dp", "seq", None),
            P("dp", "seq", None),
            P("dp", "seq", None),
            P("seq", None),
            P("dp"),
            P(),
        ),
        out_specs=(P("dp"), P("seq", "dp")),
        check_vma=False,
    )
```

time: 77.5 us -> 67.4 us (0.87)
  local copies, waits for them, and re-layouts: 7.79 us -> 0 us
  Pallas kernels: 68.8 us -> 66.6 us
    unnamed x12 -> x0, local copies, waits for them, and re-layouts: 7.13 us -> none
    pallas_call x1 -> x2, Pallas kernels: 68.8 us -> 66.6 us  [the longest x1 64.2 us: shards(): pl.pallas_call(kernel, out_shape=jax.ShapeDtypeStruct((72, 256), F32), in...]
where the time goes in v2:
time: 67.4 us; the launch traced here: 67.3 us
  Pallas kernels  66.6 us (99%)
    pallas_call x1, Pallas kernels, shards(): pl.pallas_call(kernel, out_shape=jax.ShapeDtypeStruct((72, 256), F32), in...  64.2 us
    pallas_call x1, Pallas kernels, shards(): pl.pallas_call(finish, out_shape=(jax.ShapeDtypeStruct((2,), F32), jax.Sh...  2.44 us

profile of v2, /device:TPU:1, one launch (start us, length us, event | category | flops | bytes accessed | tf_op | source)
XLA Modules:
  0.0 67.3 jit_solution(17722324485498081954)
XLA Ops:
  0.6 64.2 %shard_map.86.end_ref = f32[72,256]{1,0:T(8,128)} custom-call(bf16[2,128,4096]{2,1,0:T(8,128)(2,1)} %q_hbm.1, bf16[2,128,1024]{2,1,0:T(8,128)(2,1)} %k_hbm.1, bf16[2,128,1024]{2,1,0:T(8,128)(2,1)} %v_hbm.1, bf16[2,128,4096]{2,1,0:T(8,128)(2,1)} %hid_ref.1, bf16[256,4096]{1,0:T(8,128)(2,1)} %wt_ref.1, s32[2]{0:T(128)} %len_ref.1), custom_call_target="tpu_custom_call" | custom-call | tf_op jit(solution)/shard_map/pallas_call | solution.py:394
  64.8 2.4 %shard_map.87 = (f32[2]{0:T(128)}, f32[256,256]{1,0:T(8,128)}) custom-call(f32[72,256]{1,0:T(8,128)} %shard_map.86.end_ref, s32[1,32]{1,0:T(1,128)} %bitcast.1), custom_call_target="tpu_custom_call" | custom-call | tf_op jit(solution)/shard_map/pallas_call | solution.py:430

commit v3 on v2

--- a/solution.py
+++ b/solution.py
@@ -47,12 +47,19 @@
     col = (s // 2) % 4
     row = s // 8
 
-    def seq_peer(e):
-        odd = e % 2
-        i = (e // 2) % 4
-        dc = 1 - e // 8
-        dx = (i + 3 - 2 * odd) % 4
-        return ((row + 1 - odd) % 2) * 8 + ((col + dx) % 4) * 2 + (core + dc) % 2
+    rows = [row * 8, (1 - row) * 8]
+    ring = [((col + dx) % 4) * 2 for dx in range(4)]
+    cores = [core, 1 - core]
+
+    def at(dy, dx, dc):
+        return rows[dy] + ring[dx] + cores[dc]
+
+    peers = []
+    for dc in range(2):
+        for dx in (2, 1, 0, 3):
+            peers.append(at(1, dx, dc))
+            if dc or dx != 2:
+                peers.append(at(0, (dx + 2) % 4, dc))
 
     k_copy = pltpu.make_async_copy(k_hbm, k_ref, recv_sem.at[K_IN_SEM])
     k_copy.start()
@@ -79,11 +86,8 @@
     barrier = pltpu.get_barrier_semaphore()
     signal(barrier, far_half, z_next, z_prev)
 
-    def greet(e, c):
-        signal(barrier, (g, seq_peer(e)))
-        return c
-
-    lax.fori_loop(0, RANKS - 1, greet, 0)
+    for t in peers:
+        signal(barrier, (g, t))
     pl.semaphore_wait(barrier, RANKS + 2)
 
     def remote(src, dst, sem, target):
@@ -95,26 +99,10 @@
     def cols(first):
         return pl.ds(pl.multiple_of(first * LANES, LANES), LANES)
 
-    def send_k(e, c):
-        t = seq_peer(e)
-        remote(k_ref.at[t % 2, :, cols(t // 2)], kbuf.at[s], K_SEM, (g, t))
-        return c
-
-    def send_q(h):
-        def body(e, c):
-            t = seq_peer(e)
-            remote(q_ref.at[t % 2, :, cols((t // 2) * HEADS + h)], qbuf.at[h, s], Q_SEM + h, (g, t))
-            return c
-        return body
-
-    def send_v(e, c):
-        t = seq_peer(e)
-        remote(v_ref.at[t % 2, :, cols(t // 2)], vbuf.at[s], V_SEM, (g, t))
-        return c
-
     k_copy.wait()
     pltpu.make_async_copy(k_ref.at[core, :, cols(s // 2)], kbuf.at[s], recv_sem.at[K_SEM]).start()
-    lax.fori_loop(0, RANKS - 1, send_k, 0)
+    for t in peers:
+        remote(k_ref.at[t % 2, :, cols(t // 2)], kbuf.at[s], K_SEM, (g, t))
 
     q_copy.wait()
     v_copy.wait()
@@ -123,21 +111,17 @@
         pltpu.make_async_copy(
             q_ref.at[core, :, cols((s // 2) * HEADS + h)], qbuf.at[h, s], recv_sem.at[Q_SEM + h]
         ).start()
-        lax.fori_loop(0, RANKS - 1, send_q(h), 0)
+        for t in peers:
+            remote(q_ref.at[t % 2, :, cols((t // 2) * HEADS + h)], qbuf.at[h, s], Q_SEM + h, (g, t))
         return c
 
     lax.fori_loop(0, HEADS, send_head, 0)
     pltpu.make_async_copy(v_ref.at[core, :, cols(s // 2)], vbuf.at[s], recv_sem.at[V_SEM]).start()
-    lax.fori_loop(0, RANKS - 1, send_v, 0)
+    for t in peers:
+        remote(v_ref.at[t % 2, :, cols(t // 2)], vbuf.at[s], V_SEM, (g, t))
 
     wt_copy.wait()
     remote(wbuf.at[core], wbuf.at[core], W_SEM, sibling)
-
-    for r in range(4):
-        signal(sync.at[r], z_next, z_prev)
-        pl.semaphore_wait(sync.at[r], 2)
-    signal(sync.at[4], far_half)
-    pl.semaphore_wait(sync.at[4], 1)
 
     def wait_all(ref, sem):
         pltpu.make_async_copy(ref, ref, sem).wait()
@@ -153,21 +137,17 @@
         mask = jnp.where(place < length, ones, zeros).astype(BF16)
         inv_len = jnp.full((1, 1), 1.0, F32) / jnp.full((1, 1), length, jnp.int32).astype(F32)
 
-        def add_resid(t, c, doc=doc, mask=mask, inv_len=inv_len):
-            part = jnp.dot(
-                mask, hbuf[doc, :, pl.ds(pl.multiple_of(t * 256, 256), 256)],
-                preferred_element_type=F32) * inv_len
-            resid[t, doc:doc + 1, :] = part[0:1, 0:LANES]
-            resid[t, 2 + doc:3 + doc, :] = part[0:1, LANES:]
-            return c
-
-        lax.fori_loop(0, RANKS, add_resid, 0)
+        part = jnp.dot(mask, hbuf[doc], preferred_element_type=F32)[0:1] * inv_len
+        for t in range(RANKS):
+            resid[t, doc:doc + 1, :] = part[:, 256 * t:256 * t + LANES]
+            resid[t, 2 + doc:3 + doc, :] = part[:, 256 * t + LANES:256 * t + 256]
 
     my_len = len_ref[core]
 
     wait_all(kbuf, recv_sem.at[K_SEM])
 
     def one_head(h, c):
+        signal(sync.at[h], z_next, z_prev)
         wait_all(qbuf.at[h], recv_sem.at[Q_SEM + h])
         for i in range(LEN // QB):
             n = (i + 1) * QB
@@ -207,10 +187,12 @@
             preferred_element_type=F32)
         for p, part in enumerate(split3(w_row[0:1])):
             lhs_ref[pl.ds(p * HEADS + h, 1), :] = part
+        pl.semaphore_wait(sync.at[h], 2)
         return c
 
     lhs_ref[12:16, :] = jnp.zeros((4, LEN), F32)
     lax.fori_loop(0, HEADS, one_head, 0)
+    signal(sync.at[HEADS], far_half)
     lhs = lhs_ref[...].astype(BF16)
 
     wait_all(vbuf, recv_sem.at[V_SEM])
@@ -218,27 +200,32 @@
     out = jnp.dot(lhs, vbuf[...].reshape(LEN, LANES), preferred_element_type=F32)
     mine = (out[0:4] + out[4:8] + out[8:12]) * inv_my_len
 
+    pl.semaphore_wait(sync.at[HEADS], 1)
+
     wide_mine = jnp.concatenate([mine[h:h + 1] for h in range(HEADS)], axis=1)
     lhs2 = jnp.concatenate(
         list(split3(wide_mine)) + [jnp.zeros((13, HEADS * LANES), F32)], axis=0).astype(BF16)
     wait_all(wbuf.at[0], recv_sem.at[W_SEM])
-    part = jnp.dot(
-        lhs2, wbuf[...].reshape(HEADS * LANES, 4096), preferred_element_type=F32)
-    part = part[0:1] + part[1:2] + part[2:3]
     tile_row = lax.broadcasted_iota(jnp.int32, (4, LANES), 0)
-    for t in range(RANKS):
-        rs_out[t] = resid[t] + jnp.where(
-            tile_row == core, part[:, 256 * t:256 * t + LANES],
-            jnp.where(tile_row == 2 + core, part[:, 256 * t + LANES:256 * t + 256], 0.0))
-
-    def send_partial(e, c):
-        t = seq_peer(e)
-        remote(rs_out.at[t], rs_buf.at[y_hi * RANKS + s], RS_SEM, (g, t))
-        remote(rs_out.at[t], rs_buf.at[y_hi * RANKS + s], RS_SEM, (z * 2 + 1 - y_hi, t))
-        return c
-
-    lax.fori_loop(0, RANKS - 1, send_partial, 0)
-    remote(rs_out.at[s], rs_buf.at[y_hi * RANKS + s], RS_SEM, far_half)
+
+    for dy in (1, 0):
+        part = jnp.dot(
+            lhs2,
+            wbuf[:, :, pl.ds(pl.multiple_of(rows[dy] * 256, 2048), 2048)].reshape(
+                HEADS * LANES, 2048),
+            preferred_element_type=F32)
+        part = part[0:1] + part[1:2] + part[2:3]
+        for k in range(8):
+            rs_out[rows[dy] + k] = resid[rows[dy] + k] + jnp.where(
+                tile_row == core, part[:, 256 * k:256 * k + LANES],
+                jnp.where(tile_row == 2 + core, part[:, 256 * k + LANES:256 * k + 256], 0.0))
+        for dx in (2, 1, 3, 0):
+            for dc in (1, 0):
+                t = at(dy, dx, dc)
+                mine_there = rs_buf.at[y_hi * RANKS + s]
+                remote(rs_out.at[t], mine_there, RS_SEM, (z * 2 + 1 - y_hi, t))
+                if dy or dx or dc:
+                    remote(rs_out.at[t], mine_there, RS_SEM, (g, t))
     rs_buf[y_hi * RANKS + s] = rs_out[s]
 
     sib[core] = mine
@@ -252,7 +239,7 @@
     pg_buf[g] = both
 
     def send_pooled(e, c):
-        remote(ptile, pg_buf.at[g], PG_SEM, ((g + e + 1) % RANKS, s))
+        remote(ptile, pg_buf.at[g], PG_SEM, (lax.rem(g + e + 1, RANKS), s))
         return c
 
     lax.fori_loop(0, RANKS - 1, send_pooled, 0)
@@ -263,11 +250,8 @@
         rtile[half] = raw
         rg_buf[z, half] = raw
 
-    def send_raw(e, c):
-        remote(rtile, rg_buf.at[z], RG_SEM, (((z + e + 1) % 8) * 2 + y_hi, s))
-        return c
-
-    lax.fori_loop(0, 7, send_raw, 0)
+    for dz in (4, 3, 5, 2, 6, 1, 7):
+        remote(rtile, rg_buf.at[z], RG_SEM, (((z + dz) % 8) * 2 + y_hi, s))
 
     @pl.when(s == g)
     def _():
@@ -297,11 +281,8 @@
     gtile[...] = packed
     gram_buf[s] = packed
 
-    def send_gram(e, c):
-        remote(gtile, gram_buf.at[s], GRAM_SEM, (g, seq_peer(e)))
-        return c
-
-    lax.fori_loop(0, RANKS - 1, send_gram, 0)
+    for t in peers:
+        remote(gtile, gram_buf.at[s], GRAM_SEM, (g, t))
 
     wait_all(pg_buf.at[pl.ds(0, RANKS - 1)], recv_sem.at[PG_SEM])
     for d in range(RANKS):
@@ -425,7 +406,7 @@
             pltpu.SemaphoreType.REGULAR((5,)),
         ],
         compiler_params=pltpu.CompilerParams(
-            collective_id=0, has_side_effects=True, vmem_limit_bytes=60 * 2**20),
+            collective_id=0, has_side_effects=True, vmem_limit_bytes=107 * 2**19),
     )(q_proj, k_proj, v_proj, hidden_in, out_weight, doc_lengths)
     return pl.pallas_call(
         finish,
@@ -435,7 +416,7 @@
         ),
         in_specs=[vmem] * 2,
         out_specs=(smem, vmem),
-        compiler_params=pltpu.CompilerParams(vmem_limit_bytes=60 * 2**20),
+        compiler_params=pltpu.CompilerParams(vmem_limit_bytes=107 * 2**19),
     )(end, positive.reshape(1, 32))
 
 

time: 67.4 us -> 65.3 us (0.969)
  Pallas kernels: 66.6 us -> 63.9 us
    pallas_call x1, Pallas kernels: 64.2 us -> 62.3 us  [shards(): pl.pallas_call(kernel, out_shape=jax.ShapeDtypeStruct((72, 256), F32), in...]
    pallas_call x1, Pallas kernels: 2.44 us -> 1.55 us  [shards(): pl.pallas_call(finish, out_shape=(jax.ShapeDtypeStruct((2,), F32), jax.Sh...]
where the time goes in v3:
time: 65.3 us; the launch traced here: 65.2 us
  Pallas kernels  63.9 us (98%)
  between operations  0.66 us (1%)
    pallas_call x1, Pallas kernels, shards(): pl.pallas_call(kernel, out_shape=jax.ShapeDtypeStruct((72, 256), F32), in...  62.3 us
    pallas_call x1, Pallas kernels, shards(): pl.pallas_call(finish, out_shape=(jax.ShapeDtypeStruct((2,), F32), jax.Sh...  1.55 us

profile of v3, /device:TPU:1, one launch (start us, length us, event | category | flops | bytes accessed | tf_op | source)
XLA Modules:
  0.0 65.2 jit_solution(17813057080806544242)
XLA Ops:
  0.6 0.0 copy-start
  0.6 0.6 copy-done
  1.3 0.0 copy-start.1
  1.3 62.3 %shard_map.86.end_ref = f32[72,256]{1,0:T(8,128)S(1)} custom-call(bf16[2,128,4096]{2,1,0:T(8,128)(2,1)} %q_hbm.1, bf16[2,128,1024]{2,1,0:T(8,128)(2,1)} %k_hbm.1, bf16[2,128,1024]{2,1,0:T(8,128)(2,1)} %v_hbm.1, bf16[2,128,4096]{2,1,0:T(8,128)(2,1)} %hid_ref.1, bf16[256,4096]{1,0:T(8,128)(2,1)} %wt_ref.1, s32[2]{0:T(128)S(1)} %copy-done), custom_call_target="tpu_custom_call" | custom-call | tf_op jit(solution)/shard_map/pallas_call | solution.py:375
  63.6 0.0 copy-done.1
  63.6 1.6 %shard_map.87 = (f32[2]{0:T(128)}, f32[256,256]{1,0:T(8,128)}) custom-call(f32[72,256]{1,0:T(8,128)S(1)} %shard_map.86.end_ref, s32[1,32]{1,0:T(1,128)S(1)} %bitcast.1), custom_call_target="tpu_custom_call" | custom-call | tf_op jit(solution)/shard_map/pallas_call | solution.py:411
Async XLA Ops:
  0.6 0.7 %copy-start = (s32[2]{0:T(128)S(1)}, s32[2]{0:T(128)}, u32[]{:S(2)}) copy-start(s32[2]{0:T(128)} %len_ref.1) | copy-start | bytes 28
  1.3 62.3 %copy-start.1 = (s32[32]{0:T(128)S(1)}, s32[32]{0:T(128)}, u32[]{:S(2)}) copy-start(s32[32]{0:T(128)} %param.13) | copy-start | bytes 388

commit v4 on v3

--- a/solution.py
+++ b/solution.py
@@ -61,6 +61,22 @@
             if dc or dx != 2:
                 peers.append(at(0, (dx + 2) % 4, dc))
 
+    z = g // 2
+    y_hi = g % 2
+    sibling = (g, s + 1 - 2 * core)
+    z_next = (((z + 1) % 8) * 2 + y_hi, s)
+    z_prev = (((z + 7) % 8) * 2 + y_hi, s)
+    far_half = (z * 2 + 1 - y_hi, s)
+
+    def signal(sem, *targets):
+        for target in targets:
+            pl.semaphore_signal(sem, inc=1, device_id=target, device_id_type=MESH)
+
+    barrier = pltpu.get_barrier_semaphore()
+    for t in peers:
+        signal(barrier, (g, t))
+    signal(barrier, far_half, z_next, z_prev)
+
     k_copy = pltpu.make_async_copy(k_hbm, k_ref, recv_sem.at[K_IN_SEM])
     k_copy.start()
     q_copy = pltpu.make_async_copy(q_hbm, q_ref, recv_sem.at[Q_IN_SEM])
@@ -72,22 +88,6 @@
     wt_copy = pltpu.make_async_copy(wt_ref, wbuf.at[core], recv_sem.at[W_IN_SEM])
     wt_copy.start()
 
-    z = g // 2
-    y_hi = g % 2
-    sibling = (g, s + 1 - 2 * core)
-    z_next = (((z + 1) % 8) * 2 + y_hi, s)
-    z_prev = (((z + 7) % 8) * 2 + y_hi, s)
-    far_half = (z * 2 + 1 - y_hi, s)
-
-    def signal(sem, *targets):
-        for target in targets:
-            pl.semaphore_signal(sem, inc=1, device_id=target, device_id_type=MESH)
-
-    barrier = pltpu.get_barrier_semaphore()
-    signal(barrier, far_half, z_next, z_prev)
-
-    for t in peers:
-        signal(barrier, (g, t))
     pl.semaphore_wait(barrier, RANKS + 2)
 
     def remote(src, dst, sem, target):
@@ -100,12 +100,11 @@
         return pl.ds(pl.multiple_of(first * LANES, LANES), LANES)
 
     k_copy.wait()
-    pltpu.make_async_copy(k_ref.at[core, :, cols(s // 2)], kbuf.at[s], recv_sem.at[K_SEM]).start()
     for t in peers:
         remote(k_ref.at[t % 2, :, cols(t // 2)], kbuf.at[s], K_SEM, (g, t))
+    pltpu.make_async_copy(k_ref.at[core, :, cols(s // 2)], kbuf.at[s], recv_sem.at[K_SEM]).start()
 
     q_copy.wait()
-    v_copy.wait()
 
     def send_head(h, c):
         pltpu.make_async_copy(
@@ -116,6 +115,7 @@
         return c
 
     lax.fori_loop(0, HEADS, send_head, 0)
+    v_copy.wait()
     pltpu.make_async_copy(v_ref.at[core, :, cols(s // 2)], vbuf.at[s], recv_sem.at[V_SEM]).start()
     for t in peers:
         remote(v_ref.at[t % 2, :, cols(t // 2)], vbuf.at[s], V_SEM, (g, t))
@@ -230,6 +230,28 @@
 
     sib[core] = mine
     remote(sib.at[core], sib.at[core], SIB_SEM, sibling)
+
+    wait_all(rs_buf.at[pl.ds(0, 2 * RANKS - 1)], recv_sem.at[RS_SEM])
+    for half in range(2):
+        raw = jnp.sum(rs_buf[half * RANKS:(half + 1) * RANKS], axis=0)
+        rtile[half] = raw
+        rg_buf[z, half] = raw
+
+    for dz in (4, 3, 5, 2, 6, 1, 7):
+        remote(rtile, rg_buf.at[z], RG_SEM, (((z + dz) % 8) * 2 + y_hi, s))
+
+    @pl.when(s == g)
+    def _():
+        tg_buf[g] = rtile[y_hi]
+
+    def send_cols(e, c):
+        @pl.when(jnp.logical_or(s != g, e != s))
+        def _():
+            remote(rtile.at[y_hi], tg_buf.at[g], TG_SEM, (s, e))
+        return c
+
+    lax.fori_loop(0, RANKS, send_cols, 0)
+
     wait_all(sib.at[0], recv_sem.at[SIB_SEM])
     low = core == 0
     doc0 = jnp.where(low, sib[0, 0:2, :], sib[0, 2:4, :])
@@ -243,27 +265,6 @@
         return c
 
     lax.fori_loop(0, RANKS - 1, send_pooled, 0)
-
-    wait_all(rs_buf.at[pl.ds(0, 2 * RANKS - 1)], recv_sem.at[RS_SEM])
-    for half in range(2):
-        raw = jnp.sum(rs_buf[half * RANKS:(half + 1) * RANKS], axis=0)
-        rtile[half] = raw
-        rg_buf[z, half] = raw
-
-    for dz in (4, 3, 5, 2, 6, 1, 7):
-        remote(rtile, rg_buf.at[z], RG_SEM, (((z + dz) % 8) * 2 + y_hi, s))
-
-    @pl.when(s == g)
-    def _():
-        tg_buf[g] = rtile[y_hi]
-
-    def send_cols(e, c):
-        @pl.when(jnp.logical_or(s != g, e != s))
-        def _():
-            remote(rtile.at[y_hi], tg_buf.at[g], TG_SEM, (s, e))
-        return c
-
-    lax.fori_loop(0, RANKS, send_cols, 0)
 
     wait_all(rg_buf.at[pl.ds(0, 7)], recv_sem.at[RG_SEM])
     for d in range(RANKS):
@@ -359,9 +360,12 @@
     along = jnp.sum(weighted * gram, axis=1, keepdims=True)
     coef = inv_i * weighted - eye_f * (inv_i * along / sq_i)
     grad_raw = jnp.dot(coef, raw, precision=HIGHEST, preferred_element_type=F32)
+    ph, pm, pl_ = split3(pooled)
+    gh, gm, gl = split3(grad_raw)
+    left = jnp.concatenate([ph, ph, pm, pm, ph, pl_], axis=0).astype(BF16)
+    right = jnp.concatenate([gh, gm, gh, gm, gl, gh], axis=0).astype(BF16)
     wo_ref[...] = lax.dot_general(
-        pooled, grad_raw, (((0,), (0,)), ((), ())), precision=HIGHEST,
-        preferred_element_type=F32)
+        left, right, (((0,), (0,)), ((), ())), preferred_element_type=F32)
     doc_at = lax.broadcasted_iota(jnp.int32, (32, 1), 0)
     cost_ref[0] = jnp.sum(jnp.where(doc_at == 2 * g, cost, 0.0))
     cost_ref[1] = jnp.sum(jnp.where(doc_at == 2 * g + 1, cost, 0.0))

time: 65.3 us -> 64.9 us (level)
  no operation moved by 1% of the time
where the time goes in v4:
time: 64.9 us; the launch traced here: 64.8 us
  Pallas kernels  63.5 us (98%)
  between operations  0.66 us (1%)
  local copies, waits for them, and re-layouts  0.65 us (1%)
    pallas_call x1, Pallas kernels, shards(): pl.pallas_call(kernel, out_shape=jax.ShapeDtypeStruct((72, 256), F32), in...  62.1 us
    pallas_call x1, Pallas kernels, shards(): pl.pallas_call(finish, out_shape=(jax.ShapeDtypeStruct((2,), F32), jax.Sh...  1.4 us

profile of v4, /device:TPU:1, one launch (start us, length us, event | category | flops | bytes accessed | tf_op | source)
XLA Modules:
  0.0 64.8 jit_solution(12699170797298405925)
XLA Ops:
  0.6 0.0 copy-start
  0.6 0.6 copy-done
  1.3 0.0 copy-start.1
  1.3 62.1 %shard_map.86.end_ref = f32[72,256]{1,0:T(8,128)S(1)} custom-call(bf16[2,128,4096]{2,1,0:T(8,128)(2,1)} %q_hbm.1, bf16[2,128,1024]{2,1,0:T(8,128)(2,1)} %k_hbm.1, bf16[2,128,1024]{2,1,0:T(8,128)(2,1)} %v_hbm.1, bf16[2,128,4096]{2,1,0:T(8,128)(2,1)} %hid_ref.1, bf16[256,4096]{1,0:T(8,128)(2,1)} %wt_ref.1, s32[2]{0:T(128)S(1)} %copy-done), custom_call_target="tpu_custom_call" | custom-call | tf_op jit(solution)/shard_map/pallas_call | solution.py:379
  63.4 0.0 copy-done.1
  63.4 1.4 %shard_map.87 = (f32[2]{0:T(128)}, f32[256,256]{1,0:T(8,128)}) custom-call(f32[72,256]{1,0:T(8,128)S(1)} %shard_map.86.end_ref, s32[1,32]{1,0:T(1,128)S(1)} %bitcast.1), custom_call_target="tpu_custom_call" | custom-call | tf_op jit(solution)/shard_map/pallas_call | solution.py:415
Async XLA Ops:
  0.6 0.7 %copy-start = (s32[2]{0:T(128)S(1)}, s32[2]{0:T(128)}, u32[]{:S(2)}) copy-start(s32[2]{0:T(128)} %len_ref.1) | copy-start | bytes 28
  1.3 62.1 %copy-start.1 = (s32[32]{0:T(128)S(1)}, s32[32]{0:T(128)}, u32[]{:S(2)}) copy-start(s32[32]{0:T(128)} %param.13) | copy-start | bytes 388

commit v5 on v4

--- a/solution.py
+++ b/solution.py
@@ -270,8 +270,9 @@
     for d in range(RANKS):
         for half in range(2):
             piece = rg_buf[d // 2, d % 2, 2 * half:2 * half + 2, :]
-            for rep in range(4):
-                rg_mat[32 * rep + 2 * d:32 * rep + 2 * d + 2, half * LANES:(half + 1) * LANES] = piece
+            rg_mat[2 * d:2 * d + 2, half * LANES:(half + 1) * LANES] = piece
+    for rep in range(1, 4):
+        rg_mat[32 * rep:32 * rep + 32, :] = rg_mat[0:32, :]
     wide = lax.dot_general(
         rg_mat[0:32, :], rg_mat[...], (((1,), (1,)), ((), ())), precision=HIGHEST,
         preferred_element_type=F32)
@@ -304,11 +305,6 @@
             end_ref[32 + 2 * d:34 + 2 * d, half * LANES:(half + 1) * LANES] = tg_buf[
                 d, 2 * half:2 * half + 2, :]
 
-    wait_all(gram_buf.at[pl.ds(0, RANKS - 1)], recv_sem.at[GRAM_SEM])
-    gp = jnp.sum(gram_buf[...], axis=0)
-    end_ref[64:72, 0:LANES] = gp
-    end_ref[64:72, LANES:] = gp
-
     some = RANKS - 1
     wait_all(kbuf.at[pl.ds(0, some)], send_sem.at[K_SEM])
     for h in range(HEADS):
@@ -328,7 +324,13 @@
         wait_all(tg_buf, send_sem.at[TG_SEM])
 
     wait_all(pg_buf.at[pl.ds(0, some)], send_sem.at[PG_SEM])
-    wait_all(gram_buf.at[pl.ds(0, some)], send_sem.at[GRAM_SEM])
+
+    wait_all(gram_buf.at[pl.ds(0, RANKS - 1)], recv_sem.at[GRAM_SEM])
+    gp = jnp.sum(gram_buf[...], axis=0)
+    end_ref[64:72, 0:LANES] = gp
+    end_ref[64:72, LANES:] = gp
+
+    wait_all(gram_buf.at[pl.ds(0, RANKS - 1)], send_sem.at[GRAM_SEM])
 
 
 def finish(end_ref, pos_ref, cost_ref, wo_ref):

time: 64.9 us -> 64.9 us (level)
  no operation moved by 1% of the time
where the time goes in v5:
time: 64.9 us; the launch traced here: 64.8 us
  Pallas kernels  63.5 us (98%)
  between operations  0.66 us (1%)
  local copies, waits for them, and re-layouts  0.65 us (1%)
    pallas_call x1, Pallas kernels, shards(): pl.pallas_call(kernel, out_shape=jax.ShapeDtypeStruct((72, 256), F32), in...  62.1 us
    pallas_call x1, Pallas kernels, shards(): pl.pallas_call(finish, out_shape=(jax.ShapeDtypeStruct((2,), F32), jax.Sh...  1.4 us

profile of v5, /device:TPU:1, one launch (start us, length us, event | category | flops | bytes accessed | tf_op | source)
XLA Modules:
  0.0 64.8 jit_solution(16417049588041897644)
XLA Ops:
  0.6 0.0 copy-start
  0.6 0.6 copy-done
  1.3 0.0 copy-start.1
  1.3 62.1 %shard_map.86.end_ref = f32[72,256]{1,0:T(8,128)S(1)} custom-call(bf16[2,128,4096]{2,1,0:T(8,128)(2,1)} %q_hbm.1, bf16[2,128,1024]{2,1,0:T(8,128)(2,1)} %k_hbm.1, bf16[2,128,1024]{2,1,0:T(8,128)(2,1)} %v_hbm.1, bf16[2,128,4096]{2,1,0:T(8,128)(2,1)} %hid_ref.1, bf16[256,4096]{1,0:T(8,128)(2,1)} %wt_ref.1, s32[2]{0:T(128)S(1)} %copy-done), custom_call_target="tpu_custom_call" | custom-call | tf_op jit(solution)/shard_map/pallas_call | solution.py:381
  63.4 0.0 copy-done.1
  63.4 1.4 %shard_map.87 = (f32[2]{0:T(128)}, f32[256,256]{1,0:T(8,128)}) custom-call(f32[72,256]{1,0:T(8,128)S(1)} %shard_map.86.end_ref, s32[1,32]{1,0:T(1,128)S(1)} %bitcast.1), custom_call_target="tpu_custom_call" | custom-call | tf_op jit(solution)/shard_map/pallas_call | solution.py:417
Async XLA Ops:
  0.6 0.7 %copy-start = (s32[2]{0:T(128)S(1)}, s32[2]{0:T(128)}, u32[]{:S(2)}) copy-start(s32[2]{0:T(128)} %len_ref.1) | copy-start | bytes 28
  1.3 62.1 %copy-start.1 = (s32[32]{0:T(128)S(1)}, s32[32]{0:T(128)}, u32[]{:S(2)}) copy-start(s32[32]{0:T(128)} %param.13) | copy-start | bytes 388
